TPU v7x, 32 devices: a whole 2x2x4 slice. The times are simulated.
32 devices in a mesh: dom: 8 (over y, x, core), rep: 4 (over z).
Axes of the slice: x: 2, y: 2, z: 4, core: 2. Of those that a mesh axis runs over, the one named last changes fastest.
Arguments:
- features: float32 [2048, 256], P('dom'), may hold values from -6 to 6
- tile_values: bfloat16 [8, 64, 128, 128], P('dom', 'rep'), may hold values from 0 to 0.03125
- tile_rows: int32 [8, 64], P('dom', 'rep'), may hold values from 0 to 1
- tile_cols: int32 [8, 64], P('dom', 'rep'), may hold values from 0 to 15, as said below
- weight: float32 [256, 256], replicated, may hold values from -0.375 to 0.375
- bias: float32 [256], replicated, may hold values from -3 to 3
- cotangent: float32 [2048, 256], P('dom'), may hold values from -6 to 6
Outputs:
- activations: float32 [2048, 256], P('dom')
- grad_features: float32 [2048, 256], P('dom')
- grad_weight: float32 [256, 256], replicated
- grad_bias: float32 [256], replicated
Inputs may be any that keep to these rules, and one draw needn't show every extreme that they name: `tile_cols`: within each share of 16 consecutive tiles of a partition, every tile column 0 to 15 appears exactly once.
All inputs are finite; a program needn't handle non-finite values.
Results may differ from a plain program's by a relative error of at most 0.0003.
Values sent between devices are 32-bit elements; how exact they have to be, the bound alone decides.
A program may use at most 64 MiB of HBM per device.

v0:
```python
import jax
import jax.numpy as jnp
from jax import lax
from jax.sharding import PartitionSpec as P


def body(features, tile_values, tile_rows, tile_cols, weight, bias, cotangent):
    highest = lax.Precision.HIGHEST
    values = tile_values[0].astype(jnp.float32)
    row_ids = tile_rows[0]
    col_ids = tile_cols[0]
    tile_size = values.shape[1]
    node_rows = features.shape[0]
    feat_width = features.shape[1]
    row_blocks = node_rows // tile_size
    shard_piece = lax.all_gather(features, "dom", axis=0, tiled=True)
    block_count = shard_piece.shape[0] // tile_size
    blocks = shard_piece.reshape(block_count, tile_size, feat_width)
    offsets = col_ids[:, None]
    select = (offsets == jnp.arange(block_count, dtype=jnp.int32)[None, :]).astype(jnp.float32)
    selected = jnp.einsum("sn,nif->sif", select, blocks, precision=highest)
    products = jnp.einsum("sij,sjf->sif", values, selected, precision=highest)
    row_select = (row_ids[None, :] == jnp.arange(row_blocks, dtype=jnp.int32)[:, None]).astype(
        jnp.float32
    )
    partial_rows = jnp.einsum("bs,sif->bif", row_select, products, precision=highest).reshape(
        node_rows, feat_width
    )
    aggregated = lax.psum(partial_rows, "rep")
    before = jnp.dot(aggregated, weight, precision=highest) + bias
    gate_value = jax.nn.sigmoid(before)
    output = before * gate_value
    grad_pre = cotangent * gate_value * (1.0 + before * (1.0 - gate_value))
    messages = jnp.dot(grad_pre, weight.T, precision=highest)
    weight_term = jnp.dot(aggregated.T, grad_pre, precision=highest)
    activations, messages, weight_term, bias_term = (
        output,
        messages,
        weight_term,
        jnp.sum(grad_pre, axis=0),
    )
    grad_weight, grad_bias = lax.psum((weight_term, bias_term), "dom")
    message_blocks = messages.reshape(row_blocks, tile_size, feat_width)
    picked_messages = jnp.einsum("bs,bif->sif", row_select, message_blocks, precision=highest)
    returned = jnp.einsum("sji,sjf->sif", values, picked_messages, precision=highest)
    block_count = node_rows * lax.axis_size("dom") // tile_size
    offsets = col_ids[None, :]
    select = (offsets == jnp.arange(block_count, dtype=jnp.int32)[:, None]).astype(jnp.float32)
    source_part = lax.psum_scatter(
        jnp.einsum("ns,sif->nif", select, returned, precision=highest).reshape(
            node_rows * lax.axis_size("dom"), feat_width
        ),
        "dom",
        scatter_dimension=0,
        tiled=True,
    )
    grad_features = lax.psum(source_part, "rep")
    return (activations, grad_features, grad_weight, grad_bias)


def solution(mesh):
    return jax.shard_map(
        body,
        mesh=mesh,
        in_specs=(
            P("dom", None),
            P("dom", "rep", None, None),
            P("dom", "rep"),
            P("dom", "rep"),
            P(),
            P(),
            P("dom", None),
        ),
        out_specs=(P("dom", None), P("dom", None), P(), P()),
        check_vma=False,
    )
```

profile of v0, /device:TPU:0, one launch (start us, length us, event | category | flops | bytes accessed | tf_op | source)
XLA Modules:
  0.0 246.7 jit_solution(1948898299063535947)
XLA Ops:
  7.2 0.0 copy-start
  7.2 0.0 all-gather.2.cloned.1.call-start
  7.2 0.7 all-gather.2.cloned.1.call-update
  7.9 0.0 all-reduce.4.cloned.1.call-start
  8.0 32.6 %all-gather.2.cloned.1.call-done = f32[2048,256]{1,0:T(8,128)} async-done(((f32[256,256]{1,0:T(8,128)}), f32[2048,256]{1,0:T(8,128)}) %all-gather.2.cloned.1.call-update) | async-done | bytes 2097168 | tf_op jit(solution)/shard_map/all_gather | solution.py:16
  40.5 3.9 %fusion.8 = f32[16,128,256]{2,0,1:T(8,128)S(1)} fusion(f32[16,128,256]{2,1,0:T(8,128)} %bitcast.35, s32[16]{0:T(128)} %bitcast.40), kind=kOutput, calls=%fused_computation.8 | convolution fusion | flops 100663552 | bytes 4194368 | tf_op jit(solution)/shard_map/sn,nif->sif/dot_general | solution.py:21
  44.5 0.0 copy-done
  44.5 4.1 %fusion.6 = f32[16,256,128]{2,1,0:T(8,128)} fusion(f32[16,128,256]{2,0,1:T(8,128)S(1)} %fusion.8, bf16[1,16,128,128]{3,2,1,0:T(8,128)(2,1)S(1)} %copy-done), kind=kOutput, calls=%fused_computation.6 | convolution fusion | flops 805306368 | bytes 4718592 | tf_op jit(solution)/shard_map/sij,sjf->sif/dot_general | solution.py:22
  48.5 0.0 copy-start.3
  48.5 2.2 copy.15
  50.8 0.0 copy-start.1
  50.8 0.0 copy-start.5
  50.8 0.0 copy-start.6
  50.8 0.0 copy-done.3
  50.8 0.8 fusion.2
  51.6 0.7 copy.11
  52.4 0.0 all-reduce.4.cloned.1.call-update
  52.4 0.2 reduce-scatter.2.cloned.1.call-start
  52.6 35.2 %all-reduce.4.cloned.1.call-done = f32[256,256]{1,0:T(8,128)} async-done(((f32[256,256]{1,0:T(8,128)}), f32[256,256]{1,0:T(8,128)}) %all-reduce.4.cloned.1.call-update) | async-done | bytes 262160 | tf_op jit(solution)/shard_map/psum | solution.py:29
  87.9 0.0 copy-done.1
  87.9 0.0 copy-done.5
  87.9 0.0 copy-done.6
  87.9 2.1 fusion.25
  90.0 0.4 fusion.26
  90.4 1.1 fusion.12
  91.5 2.7 %fusion.4 = f32[16,256,128]{2,1,0:T(8,128)S(1)} fusion(f32[16,128,256]{2,0,1:T(8,128)S(1)} %fusion.12, bf16[1,16,128,128]{3,2,1,0:T(8,128)(2,1)S(1)} %copy-done), kind=kOutput, calls=%fused_computation.4 | convolution fusion | flops 805306368 | bytes 4718592 | tf_op jit(solution)/shard_map/sji,sjf->sif/dot_general | solution.py:45
  94.3 0.0 copy-start.4
  94.3 2.1 copy.18
  96.4 0.0 copy-done.4
  96.4 2.7 %fusion = f32[16,128,256]{2,0,1:T(8,128)S(1)} fusion(f32[16,256,128]{1,0,2:T(8,128)} %copy.18, s32[16]{0:T(128)S(1)} %bitcast.41), kind=kOutput, calls=%fused_computation | convolution fusion | flops 100663552 | bytes 4194368 | tf_op jit(solution)/shard_map/ns,sif->nif/dot_general | solution.py:50
  99.1 2.6 %copy.12 = f32[16,128,256]{2,1,0:T(8,128)} copy(f32[16,128,256]{2,0,1:T(8,128)S(1)} %fusion) | data formatting | bytes 4194304 | tf_op jit(solution)/shard_map/ns,sif->nif/dot_general | solution.py:50
  101.6 0.0 copy-start.2
  101.6 0.0 reduce-scatter.2.cloned.1.call-update
  101.6 0.0 all-reduce.8.cloned.1.call-start
  101.7 0.9 copy-done.2
  102.6 1.3 fusion.27
  103.9 0.0 all-reduce.8.cloned.1.call-update
  103.9 0.0 all-reduce.6.cloned.1.call-start
  103.9 38.8 %reduce-scatter.2.cloned.1.call-done = f32[256,256]{1,0:T(8,128)} async-done(((f32[2048,256]{1,0:T(8,128)}), f32[256,256]{1,0:T(8,128)}) %reduce-scatter.2.cloned.1.call-update) | async-done | bytes 262160 | tf_op jit(solution)/shard_map/reduce_scatter | solution.py:49
  142.8 0.0 all-reduce.6.cloned.1.call-update
  142.8 13.2 %psum.31 = f32[256]{0:T(256)} all-reduce(f32[256]{0:T(256)S(1)} %get-tuple-element.4), channel_id=1, replica_groups=mesh['dom'=8,'rep'=4] {'dom'}, use_global_device_ids=true, to_apply=%region_5.0 | all-reduce | flops 256 | bytes 2048 | tf_op jit(solution)/shard_map/psum | solution.py:42
  156.0 43.8 %all-reduce.8.cloned.1.call-done = f32[256,256]{1,0:T(8,128)} async-done(((f32[256,256]{1,0:T(8,128)}), f32[256,256]{1,0:T(8,128)}) %all-reduce.8.cloned.1.call-update) | async-done | bytes 262160 | tf_op jit(solution)/shard_map/psum | solution.py:42
  199.8 37.0 %all-reduce.6.cloned.1.call-done = f32[256,256]{1,0:T(8,128)} async-done(((f32[256,256]{1,0:T(8,128)}), f32[256,256]{1,0:T(8,128)}) %all-reduce.6.cloned.1.call-update) | async-done | bytes 262160 | tf_op jit(solution)/shard_map/psum | solution.py:57
  236.8 1.7 copy.30
  238.5 1.7 copy.31
Async XLA Ops:
  7.2 37.3 %copy-start = (bf16[1,16,128,128]{3,2,1,0:T(8,128)(2,1)S(1)}, bf16[1,16,128,128]{3,2,1,0:T(8,128)(2,1)}, u32[]{:S(2)}) copy-start(bf16[1,16,128,128]{3,2,1,0:T(8,128)(2,1)} %param.8) | copy-start | bytes 1572868
  7.2 33.4 %all-gather.2.cloned.1.call-start = ((), (), s32[]{:S(2)}) async-start(), calls=%async_computation.1 | async-start | bytes 2359296 | tf_op jit(solution)/shard_map/all_gather | solution.py:16
  7.9 79.9 %all-reduce.4.cloned.1.call-start = ((), (), s32[]{:S(2)}) async-start(), calls=%async_computation.2 | async-start | bytes 524288 | tf_op jit(solution)/shard_map/psum | solution.py:29
  48.5 2.3 copy-start.3
  50.8 37.1 %copy-start.1 = (f32[256,256]{1,0:T(8,128)S(1)}, f32[256,256]{1,0:T(8,128)}, u32[]{:S(2)}) copy-start(f32[256,256]{1,0:T(8,128)} %param.11) | copy-start | bytes 786436
  50.8 37.0 %copy-start.5 = (f32[256,256]{1,0:T(8,128)S(1)}, f32[256,256]{1,0:T(8,128)}, u32[]{:S(2)}) copy-start(f32[256,256]{1,0:T(8,128)} %param.13) | copy-start | bytes 786436
  50.8 37.0 %copy-start.6 = (f32[256]{0:T(256)S(1)}, f32[256]{0:T(256)}, u32[]{:S(2)}) copy-start(f32[256]{0:T(256)} %param.12) | copy-start | bytes 3076
  52.4 90.4 %reduce-scatter.2.cloned.1.call-start = ((), (), s32[]{:S(2)}) async-start(), calls=%async_computation.3 | async-start | bytes 2359296 | tf_op jit(solution)/shard_map/reduce_scatter | solution.py:49
  94.3 2.1 copy-start.4
  101.6 0.9 copy-start.2
  101.6 98.2 %all-reduce.8.cloned.1.call-start = ((), (), s32[]{:S(2)}) async-start(), calls=%async_computation.5 | async-start | bytes 524288 | tf_op jit(solution)/shard_map/psum | solution.py:42
  103.9 132.9 %all-reduce.6.cloned.1.call-start = ((), (), s32[]{:S(2)}) async-start(), calls=%async_computation.4 | async-start | bytes 524288 | tf_op jit(solution)/shard_map/psum | solution.py:57
Sparse Core Ops, SparseCore 0:
  9.9 30.5 all-gather.1
  52.5 35.2 all-reduce.3
  101.8 40.9 reduce-scatter.1
  146.2 53.5 all-reduce.7
  202.1 34.6 all-reduce.5
where the time goes:
time: 247 us
  waiting for transfers between devices  188 us (76%)
  matrix products  19.2 us (8%)
  between operations  13.9 us (6%)
  blocking collectives  13.2 us (5%)
  local copies, waits for them, and re-layouts  11.8 us (5%)
    psum x1, waiting for transfers between devices, body(): grad_weight, grad_bias = lax.psum((weight_term, bias_term), 'dom')  43.8 us
    reduce_scatter x1, waiting for transfers between devices, body(): lax.psum_scatter(jnp.einsum('ns,sif->nif', select, returned, precision=hi...  38.8 us
    psum x1, waiting for transfers between devices, body(): grad_features = lax.psum(source_part, 'rep')  37 us
    psum x1, waiting for transfers between devices, body(): aggregated = lax.psum(partial_rows, 'rep')  35.2 us
    all_gather x1, waiting for transfers between devices, body(): shard_piece = lax.all_gather(features, 'dom', axis=0, tiled=True)  32.6 us
    psum x1, blocking collectives, body(): grad_weight, grad_bias = lax.psum((weight_term, bias_term), 'dom')  13.2 us
  transfers between devices with their start and end apart: 5, of which 5 were waited for; matrix products, arithmetic and copies ran while one was open for 1% of the time, Pallas kernels for 0%

commit v1 on v0

--- a/solution.py
+++ b/solution.py
@@ -54,7 +54,10 @@
         scatter_dimension=0,
         tiled=True,
     )
-    grad_features = lax.psum(source_part, "rep")
+    size, grad_features = (lax.axis_size("rep"), source_part)
+    for reach in [1 << k for k in range(size.bit_length() - 1)]:
+        route = [(i, i ^ reach) for i in range(size)]
+        grad_features = grad_features + lax.ppermute(grad_features, "rep", route)
     return (activations, grad_features, grad_weight, grad_bias)
 
 

time: 247 us -> 216 us (0.87)
  waiting for transfers between devices: 188 us -> 155 us
  starting transfers between devices: 0.38 us -> 4.29 us
  local copies, waits for them, and re-layouts: 11.8 us -> 9.32 us
    psum x1 -> x0, waiting for transfers between devices: 37 us -> none  [body(): grad_features = lax.psum(source_part, 'rep')]
    ppermute x0 -> x2, waiting for transfers between devices: none -> 6.76 us  [body(): grad_features = grad_features + lax.ppermute(grad_features, 'rep', route)]
    psum x1, waiting for transfers between devices: 43.8 us -> 38.4 us  [body(): grad_weight, grad_bias = lax.psum((weight_term, bias_term), 'dom')]
    ppermute x0 -> x2, starting transfers between devices: none -> 3.95 us  [body(): grad_features = grad_features + lax.ppermute(grad_features, 'rep', route)]
    unnamed x16 -> x15, local copies, waits for them, and re-layouts: 4.25 us -> 1.71 us
  transfers between devices with their start and end apart: 5 -> 6, of which waited for: 5 -> 5; matrix products, arithmetic and copies ran while one was open for 1% -> 1% of each run, Pallas kernels for 0% -> 0%
where the time goes in v1:
time: 216 us
  waiting for transfers between devices  155 us (72%)
  matrix products  19.2 us (9%)
  between operations  13.9 us (6%)
  blocking collectives  12.6 us (6%)
  local copies, waits for them, and re-layouts  9.32 us (4%)
  starting transfers between devices  4.29 us (2%)
    reduce_scatter x1, waiting for transfers between devices, body(): lax.psum_scatter(jnp.einsum('ns,sif->nif', select, returned, precision=hi...  41.1 us
    psum x1, waiting for transfers between devices, body(): grad_weight, grad_bias = lax.psum((weight_term, bias_term), 'dom')  38.4 us
    psum x1, waiting for transfers between devices, body(): aggregated = lax.psum(partial_rows, 'rep')  35.2 us
    all_gather x1, waiting for transfers between devices, body(): shard_piece = lax.all_gather(features, 'dom', axis=0, tiled=True)  32.6 us
    psum x1, blocking collectives, body(): grad_weight, grad_bias = lax.psum((weight_term, bias_term), 'dom')  12.6 us
    ppermute x2, waiting for transfers between devices, body(): grad_features = grad_features + lax.ppermute(grad_features, 'rep', route)  6.76 us
  transfers between devices with their start and end apart: 6, of which 5 were waited for; matrix products, arithmetic and copies ran while one was open for 1% of the time, Pallas kernels for 0%

profile of v1, /device:TPU:0, one launch (start us, length us, event | category | flops | bytes accessed | tf_op | source)
XLA Modules:
  0.0 215.9 jit_solution(10446951870493001061)
XLA Ops:
  7.2 0.0 copy-start
  7.2 0.0 all-gather.2.cloned.1.call-start
  7.2 0.7 all-gather.2.cloned.1.call-update
  7.9 0.0 all-reduce.3.cloned.1.call-start
  8.0 32.6 %all-gather.2.cloned.1.call-done = f32[2048,256]{1,0:T(8,128)} async-done(((f32[256,256]{1,0:T(8,128)}), f32[2048,256]{1,0:T(8,128)}) %all-gather.2.cloned.1.call-update) | async-done | bytes 2097168 | tf_op jit(solution)/shard_map/all_gather | solution.py:16
  40.5 3.9 %fusion.8 = f32[16,128,256]{2,0,1:T(8,128)S(1)} fusion(f32[16,128,256]{2,1,0:T(8,128)} %bitcast.35, s32[16]{0:T(128)} %bitcast.40), kind=kOutput, calls=%fused_computation.8 | convolution fusion | flops 100663552 | bytes 4194368 | tf_op jit(solution)/shard_map/sn,nif->sif/dot_general | solution.py:21
  44.5 0.0 copy-done
  44.5 4.1 %fusion.6 = f32[16,256,128]{2,1,0:T(8,128)} fusion(f32[16,128,256]{2,0,1:T(8,128)S(1)} %fusion.8, bf16[1,16,128,128]{3,2,1,0:T(8,128)(2,1)S(1)} %copy-done), kind=kOutput, calls=%fused_computation.6 | convolution fusion | flops 805306368 | bytes 4718592 | tf_op jit(solution)/shard_map/sij,sjf->sif/dot_general | solution.py:22
  48.6 0.0 copy-start.3
  48.6 2.2 %copy.15 = f32[16,256,128]{1,0,2:T(8,128)S(1)} copy(f32[16,256,128]{2,1,0:T(8,128)} %fusion.6) | data formatting | bytes 4194304 | tf_op jit(solution)/shard_map/sij,sjf->sif/dot_general | solution.py:22
  50.8 0.0 copy-start.1
  50.8 0.0 copy-start.5
  50.8 0.0 copy-start.6
  50.8 0.0 copy-done.3
  50.9 0.8 fusion.2
  51.7 0.7 copy.11
  52.4 0.0 all-reduce.3.cloned.1.call-update
  52.4 0.2 reduce-scatter.2.cloned.1.call-start
  52.6 35.2 %all-reduce.3.cloned.1.call-done = f32[256,256]{1,0:T(8,128)} async-done(((f32[256,256]{1,0:T(8,128)}), f32[256,256]{1,0:T(8,128)}) %all-reduce.3.cloned.1.call-update) | async-done | bytes 262160 | tf_op jit(solution)/shard_map/psum | solution.py:29
  87.9 0.0 copy-done.1
  87.9 0.0 copy-done.5
  87.9 0.0 copy-done.6
  87.9 2.1 fusion.25
  90.0 0.4 fusion.26
  90.4 1.1 fusion.12
  91.6 2.7 %fusion.4 = f32[16,256,128]{2,1,0:T(8,128)S(1)} fusion(f32[16,128,256]{2,0,1:T(8,128)S(1)} %fusion.12, bf16[1,16,128,128]{3,2,1,0:T(8,128)(2,1)S(1)} %copy-done), kind=kOutput, calls=%fused_computation.4 | convolution fusion | flops 805306368 | bytes 4718592 | tf_op jit(solution)/shard_map/sji,sjf->sif/dot_general | solution.py:45
  94.3 0.0 copy-start.4
  94.3 2.1 copy.18
  96.4 0.0 copy-done.4
  96.4 2.7 %fusion = f32[16,128,256]{2,0,1:T(8,128)S(1)} fusion(f32[16,256,128]{1,0,2:T(8,128)} %copy.18, s32[16]{0:T(128)S(1)} %bitcast.41), kind=kOutput, calls=%fused_computation | convolution fusion | flops 100663552 | bytes 4194368 | tf_op jit(solution)/shard_map/ns,sif->nif/dot_general | solution.py:50
  99.1 2.6 %copy.12 = f32[16,128,256]{2,1,0:T(8,128)} copy(f32[16,128,256]{2,0,1:T(8,128)S(1)} %fusion) | data formatting | bytes 4194304 | tf_op jit(solution)/shard_map/ns,sif->nif/dot_general | solution.py:50
  101.6 0.0 copy-start.2
  101.6 0.0 reduce-scatter.2.cloned.1.call-update
  101.7 0.0 all-reduce.5.cloned.1.call-start
  101.7 41.1 %reduce-scatter.2.cloned.1.call-done = f32[256,256]{1,0:T(8,128)} async-done(((f32[2048,256]{1,0:T(8,128)}), f32[256,256]{1,0:T(8,128)}) %reduce-scatter.2.cloned.1.call-update) | async-done | bytes 262160 | tf_op jit(solution)/shard_map/reduce_scatter | solution.py:49
  142.8 1.5 collective-permute-start
  144.3 6.8 %collective-permute-done = f32[256,256]{1,0:T(8,128)S(1)} collective-permute-done((f32[256,256]{1,0:T(8,128)}, f32[256,256]{1,0:T(8,128)S(1)}, u32[]{:S(2)}, u32[]{:S(2)}) %collective-permute-start) | collective-permute-done | bytes 262176 | tf_op jit(solution)/shard_map/ppermute | solution.py:60
  151.1 1.0 add.32
  152.1 2.5 %collective-permute-start.1 = (f32[256,256]{1,0:T(8,128)S(1)}, f32[256,256]{1,0:T(8,128)S(1)}, u32[]{:S(2)}, u32[]{:S(2)}) collective-permute-start(f32[256,256]{1,0:T(8,128)S(1)} %add.32), channel_id=1, source_target_pairs={{0,2},{1,3},{2,0},{3,1},{4,6},{5,7},{6,4},{7,5},{8,10},{9,11},{10,... | collective-permute-start | bytes 786440 | tf_op jit(solution)/shard_map/ppermute | solution.py:60
  154.5 0.0 copy-done.2
  154.5 1.3 fusion.27
  155.8 0.0 all-reduce.5.cloned.1.call-update
  155.9 12.6 %psum.23 = f32[256]{0:T(256)} all-reduce(f32[256]{0:T(256)S(1)} %get-tuple-element.4), channel_id=1, replica_groups=mesh['dom'=8,'rep'=4] {'dom'}, use_global_device_ids=true, to_apply=%region_4.0 | all-reduce | flops 256 | bytes 2048 | tf_op jit(solution)/shard_map/psum | solution.py:42
  168.5 0.0 collective-permute-done.1
  168.5 0.7 add.33
  169.2 38.4 %all-reduce.5.cloned.1.call-done = f32[256,256]{1,0:T(8,128)} async-done(((f32[256,256]{1,0:T(8,128)}), f32[256,256]{1,0:T(8,128)}) %all-reduce.5.cloned.1.call-update) | async-done | bytes 262160 | tf_op jit(solution)/shard_map/psum | solution.py:42
  207.7 1.7 copy.29
Async XLA Ops:
  7.2 37.3 %copy-start = (bf16[1,16,128,128]{3,2,1,0:T(8,128)(2,1)S(1)}, bf16[1,16,128,128]{3,2,1,0:T(8,128)(2,1)}, u32[]{:S(2)}) copy-start(bf16[1,16,128,128]{3,2,1,0:T(8,128)(2,1)} %param.8) | copy-start | bytes 1572868
  7.2 33.4 %all-gather.2.cloned.1.call-start = ((), (), s32[]{:S(2)}) async-start(), calls=%async_computation.1 | async-start | bytes 2359296 | tf_op jit(solution)/shard_map/all_gather | solution.py:16
  7.9 80.0 %all-reduce.3.cloned.1.call-start = ((), (), s32[]{:S(2)}) async-start(), calls=%async_computation.2 | async-start | bytes 524288 | tf_op jit(solution)/shard_map/psum | solution.py:29
  48.6 2.3 %copy-start.3 = (s32[1,16]{1,0:T(1,128)S(1)}, s32[1,16]{1,0:T(1,128)}, u32[]{:S(2)}) copy-start(s32[1,16]{1,0:T(1,128)} %param.9) | copy-start | bytes 196
  50.8 37.1 %copy-start.1 = (f32[256,256]{1,0:T(8,128)S(1)}, f32[256,256]{1,0:T(8,128)}, u32[]{:S(2)}) copy-start(f32[256,256]{1,0:T(8,128)} %param.11) | copy-start | bytes 786436
  50.8 37.0 %copy-start.5 = (f32[256,256]{1,0:T(8,128)S(1)}, f32[256,256]{1,0:T(8,128)}, u32[]{:S(2)}) copy-start(f32[256,256]{1,0:T(8,128)} %param.13) | copy-start | bytes 786436
  50.8 37.0 %copy-start.6 = (f32[256]{0:T(256)S(1)}, f32[256]{0:T(256)}, u32[]{:S(2)}) copy-start(f32[256]{0:T(256)} %param.12) | copy-start | bytes 3076
  52.4 90.4 %reduce-scatter.2.cloned.1.call-start = ((), (), s32[]{:S(2)}) async-start(), calls=%async_computation.3 | async-start | bytes 2359296 | tf_op jit(solution)/shard_map/reduce_scatter | solution.py:49
  94.3 2.1 copy-start.4
  101.6 52.9 %copy-start.2 = (f32[256,256]{1,0:T(8,128)S(1)}, f32[256,256]{1,0:T(8,128)}, u32[]{:S(2)}) copy-start(f32[256,256]{1,0:T(8,128)} %all-reduce.3.cloned.1.call-done) | copy-start | bytes 786436
  101.7 106.0 %all-reduce.5.cloned.1.call-start = ((), (), s32[]{:S(2)}) async-start(), calls=%async_computation.4 | async-start | bytes 524288 | tf_op jit(solution)/shard_map/psum | solution.py:42
  142.8 8.2 %collective-permute-start = (f32[256,256]{1,0:T(8,128)}, f32[256,256]{1,0:T(8,128)S(1)}, u32[]{:S(2)}, u32[]{:S(2)}) collective-permute-start(f32[256,256]{1,0:T(8,128)} %reduce-scatter.2.cloned.1.call-done), channel_id=1, source_target_pairs={{0,1},{1,0},{2,3},{3,2},{4,5},{5,4},{6,7},{7,6},{8,9},{9,8},{10,11... | collective-permute-start | bytes 786440 | tf_op jit(solution)/shard_map/ppermute | solution.py:60
  152.1 16.4 %collective-permute-start.1 = (f32[256,256]{1,0:T(8,128)S(1)}, f32[256,256]{1,0:T(8,128)S(1)}, u32[]{:S(2)}, u32[]{:S(2)}) collective-permute-start(f32[256,256]{1,0:T(8,128)S(1)} %add.32), channel_id=1, source_target_pairs={{0,2},{1,3},{2,0},{3,1},{4,6},{5,7},{6,4},{7,5},{8,10},{9,11},{10,... | collective-permute-start | bytes 786440 | tf_op jit(solution)/shard_map/ppermute | solution.py:60
Sparse Core Ops, SparseCore 0:
  9.9 30.5 all-gather.1
  52.5 35.2 all-reduce.2
  101.8 40.9 reduce-scatter.1
  156.0 51.6 all-reduce.4
